TPU v7x, 128 devices: a whole 4x4x4 slice. The times are simulated.
128 devices in a mesh: rep: 16 (over x_lo, y, core), tp: 8 (over x_hi, z).
Axes of the slice: x: 4 (x_hi: 2, x_lo: 2; x = x_hi * 2 + x_lo), y: 4, z: 4, core: 2. Of those that a mesh axis runs over, the one named last changes fastest.
Arguments:
- tokens: bfloat16 [16, 4096, 5120], P('rep', 'tp'), may hold values from -6 to 6
- cotangent: bfloat16 [16, 4096, 1024], P('rep', 'tp'), may hold values from -6 to 6
- params: float32 [16, 5120, 1024], P('rep', 'tp'), may hold values from -0.078125 to 0.078125
- tracker: float32 [16, 5120, 1024], P('rep', 'tp'), may hold values from -6 to 6
- grad_old: float32 [16, 5120, 1024], P('rep', 'tp'), may hold values from -6 to 6
- step: int32 [1], replicated, may hold values from 0 to 2
Outputs:
- keys: bfloat16 [16, 4096, 1024], P('rep', 'tp')
- input_grad: bfloat16 [16, 4096, 5120], P('rep', 'tp')
- new_params: float32 [16, 5120, 1024], P('rep', 'tp')
- new_tracker: float32 [16, 5120, 1024], P('rep', 'tp')
All inputs are finite; a program needn't handle non-finite values.
Results may differ from a plain program's by a relative error of at most 0.009.
Values may be sent and summed in bfloat16 or wider, within the bound.
A program may use at most 128 MiB of HBM per device.

v0:
```python
from functools import partial

import jax
import jax.numpy as jnp
from jax import lax
from jax.sharding import PartitionSpec as P


def as_sent(x):

    def short(part):
        return part.astype(jnp.bfloat16) if part.dtype == jnp.float32 else part

    return jax.tree.map(short, x)


def partner(value, axis, stride):
    mask = 2**stride
    pairs = [(source, source ^ mask) for source in range(lax.axis_size(axis))]
    return lax.ppermute(value, axis, pairs)


def partner_rows(values, bit):
    return partner((as_sent(values[0]), as_sent(values[1])), "rep", bit)


def on_device(tokens, cotangent, params, tracker, grad_old, step):
    tok_rows = tokens[0]
    cot_rows = cotangent[0]
    weights = params[0].astype(jnp.bfloat16)
    contract = (((1,), (1,)), ((), ()))
    columns = tok_rows
    keys = jnp.dot(
        columns,
        lax.all_gather(weights, "tp", axis=0, tiled=True),
        preferred_element_type=jnp.float32,
    ).astype(jnp.bfloat16)
    back = lax.dot_general(
        cot_rows,
        lax.all_gather(weights, "tp", axis=0, tiled=True),
        contract,
        preferred_element_type=jnp.float32,
    ).astype(jnp.bfloat16)
    scale = 1.0 / jnp.sqrt(jnp.float32(tok_rows.shape[0] * lax.axis_size("tp")))
    columns = tok_rows
    grad = lax.psum_scatter(
        (
            lax.dot_general(
                columns, cot_rows, (((0,), (0,)), ((), ())), preferred_element_type=jnp.float32
            )
            * scale
        ).astype(jnp.bfloat16),
        "tp",
        scatter_dimension=0,
        tiled=True,
    ).astype(jnp.float32)
    half = params[0] - 0.01 * tracker[0]
    levels = lax.axis_size("rep").bit_length() - 1
    exponent = jnp.clip(step[0], 0, levels - 1)
    branches = [partial(partner_rows, bit=level) for level in range(levels)]
    half_far, tracker_far = lax.switch(exponent, branches, (half, tracker[0]))
    new_params = 0.5 * (half + half_far)
    new_tracker = 0.5 * (tracker[0] + tracker_far) + grad - grad_old[0]
    return (keys[None], back[None], new_params[None], new_tracker[None])


def solution(mesh):
    placed = (
        P("rep", "tp", None),
        P("rep", "tp", None),
        P("rep", "tp", None),
        P("rep", "tp", None),
        P("rep", "tp", None),
        P(),
    )
    return jax.shard_map(
        on_device,
        mesh=mesh,
        in_specs=placed,
        out_specs=(
            P("rep", "tp", None),
            P("rep", "tp", None),
            P("rep", "tp", None),
            P("rep", "tp", None),
        ),
        check_vma=False,
    )
```

profile of v0, /device:TPU:1, one launch (start us, length us, event | category | flops | bytes accessed | tf_op | source)
XLA Modules:
  0.0 287.2 jit_solution(9930666050806373525)
XLA Ops:
  7.2 0.0 copy-start
  7.2 0.0 all-gather.2.cloned.1.call-start
  7.2 3.1 %bitcast_convert_fusion = bf16[640,1024]{1,0:T(8,128)(2,1)} fusion(f32[1,640,1024]{2,1,0:T(8,128)} %param.12), kind=kLoop, calls=%fused_computation.15 | loop fusion | flops 655360 | bytes 3932160 | tf_op jit(solution)/shard_map/convert_element_type | solution.py:30
  10.3 0.0 all-gather.2.cloned.1.call-update
  10.3 0.0 reduce-scatter.2.cloned.1.call-start
  10.4 0.0 copy-done
  10.4 10.7 %multiply_convert_fusion = bf16[5120,1024]{1,0:T(8,128)(2,1)} fusion(bf16[1,512,5120]{2,1,0:T(8,128)(2,1)} %param.10, bf16[1,512,1024]{2,1,0:T(8,128)(2,1)S(1)} %copy-done), kind=kOutput, calls=%fused_computation | convolution fusion | flops 5379194880 | bytes 16777216 | tf_op jit(solution)/shard_map/dot_general | solution.py:48
  21.1 0.0 reduce-scatter.2.cloned.1.call-update
  21.8 0.0 copy-start.1
  21.8 5.4 %bitcast_subtract_fusion = f32[640,1024]{1,0:T(8,128)} fusion(f32[1,640,1024]{2,1,0:T(8,128)} %param.12, f32[1,640,1024]{2,1,0:T(8,128)} %param.13), kind=kLoop, calls=%fused_computation.14 | loop fusion | flops 1310720 | bytes 7864320 | tf_op jit(solution)/shard_map/sub | solution.py:57
  27.2 0.0 copy-done.1
  27.2 62.5 %conditional.4 = (bf16[640,1024]{1,0:T(8,128)(2,1)}, bf16[640,1024]{1,0:T(8,128)(2,1)}) conditional(s32[]{:T(128)} %bitcast.6, (f32[640,1024]{1,0:T(8,128)}, f32[640,1024]{1,0:T(8,128)S(1)}) %tuple.73, (f32[640,1024]{1,0:T(8,128)}, f32[640,1024]{1,0:T(8,128)S(1)}) %tuple.74, (f32[640,1024]{1,0:T(8,128)}, ...), branch_computations={%region_0.0_spmd, %region_1.2_spmd, %region_2.3_spmd, %region_3.4_... | conditional | flops 1310720 | bytes 18350176
  27.2 1.9 convert_element_type.54
  29.2 4.1 %collective-permute-start.4 = (bf16[640,1024]{1,0:T(8,128)(2,1)S(1)}, bf16[640,1024]{1,0:T(8,128)(2,1)}, u32[]{:S(2)}, u32[]{:S(2)}) collective-permute-start(bf16[640,1024]{1,0:T(8,128)(2,1)S(1)} %convert_element_type.54), channel_id=1, source_target_pairs={{0,32},{8,40},{16,48},{24,56},{32,0},{40,8},{48,16},{56,24},{64,96... | collective-permute-start | bytes 3932168 | tf_op jit(solution)/shard_map/cond/branch_2_fun/ppermute | solution.py:20
  33.3 0.2 convert_element_type.55
  33.5 0.1 collective-permute-start.5
  33.6 28.0 %collective-permute-done.4 = bf16[640,1024]{1,0:T(8,128)(2,1)} collective-permute-done((bf16[640,1024]{1,0:T(8,128)(2,1)S(1)}, bf16[640,1024]{1,0:T(8,128)(2,1)}, u32[]{:S(2)}, u32[]{:S(2)}) %collective-permute-start.4) | collective-permute-done | bytes 1310752 | tf_op jit(solution)/shard_map/cond/branch_2_fun/ppermute | solution.py:20
  61.6 28.1 %collective-permute-done.5 = bf16[640,1024]{1,0:T(8,128)(2,1)} collective-permute-done((bf16[640,1024]{1,0:T(8,128)(2,1)S(1)}, bf16[640,1024]{1,0:T(8,128)(2,1)}, u32[]{:S(2)}, u32[]{:S(2)}) %collective-permute-start.5) | collective-permute-done | bytes 1310752 | tf_op jit(solution)/shard_map/cond/branch_2_fun/ppermute | solution.py:20
  89.7 4.2 %fusion.9 = f32[1,640,1024]{2,1,0:T(8,128)} fusion(f32[640,1024]{1,0:T(8,128)} %bitcast_subtract_fusion, bf16[640,1024]{1,0:T(8,128)(2,1)} %get-tuple-element.48), kind=kLoop, calls=%fused_computation.13 | loop fusion | flops 1966080 | bytes 6553600 | tf_op jit(solution)/shard_map/broadcast_in_dim | solution.py:64
  94.0 46.0 %all-gather.2.cloned.1.call-done = bf16[5120,1024]{1,0:T(8,128)(2,1)} async-done(((bf16[640,1024]{1,0:T(8,128)(2,1)}), bf16[5120,1024]{1,0:T(8,128)(2,1)}) %all-gather.2.cloned.1.call-update) | async-done | bytes 10485776 | tf_op jit(solution)/shard_map/all_gather | solution.py:35
  139.9 0.0 copy-start.2
  139.9 11.5 %fusion = bf16[1,512,5120]{2,1,0:T(8,128)(2,1)} fusion(bf16[5120,1024]{1,0:T(8,128)(2,1)} %all-gather.2.cloned.1.call-done, bf16[1,512,1024]{2,1,0:T(8,128)(2,1)S(1)} %copy-done), kind=kOutput, calls=%fused_computation.2 | convolution fusion | flops 5371330560 | bytes 16777216 | tf_op jit(solution)/shard_map/dot_general | solution.py:38
  151.4 0.0 copy-done.2
  151.4 8.8 %fusion.13 = bf16[1,512,1024]{2,1,0:T(8,128)(2,1)} fusion(bf16[5120,1024]{1,0:T(8,128)(2,1)S(1)} %copy-done.2, bf16[1,512,5120]{2,1,0:T(8,128)(2,1)} %param.10), kind=kOutput, calls=%fused_computation.17 | convolution fusion | flops 5369233408 | bytes 16777216 | tf_op jit(solution)/shard_map/dot_general | solution.py:33
  160.2 114.3 %reduce-scatter.2.cloned.1.call-done = bf16[640,1024]{1,0:T(8,128)(2,1)} async-done(((bf16[5120,1024]{1,0:T(8,128)(2,1)}), bf16[640,1024]{1,0:T(8,128)(2,1)}) %reduce-scatter.2.cloned.1.call-update) | async-done | bytes 1310736 | tf_op jit(solution)/shard_map/reduce_scatter | solution.py:46
  274.5 5.8 %fusion.7 = f32[1,640,1024]{2,1,0:T(8,128)} fusion(bf16[640,1024]{1,0:T(8,128)(2,1)} %get-tuple-element.49, f32[1,640,1024]{2,1,0:T(8,128)} %param.14, bf16[640,1024]{1,0:T(8,128)(2,1)} %reduce-scatter.2.cloned.1.call-done, f32[1,640,1024]{2,1,0:T(8,128)} %param.13), kind=kLoop, calls=%fused_computation.10 | loop fusion | flops 3932160 | bytes 10485760 | tf_op jit(solution)/shard_map/broadcast_in_dim | solution.py:64
Async XLA Ops:
  7.2 3.2 %copy-start = (bf16[1,512,1024]{2,1,0:T(8,128)(2,1)S(1)}, bf16[1,512,1024]{2,1,0:T(8,128)(2,1)}, u32[]{:S(2)}) copy-start(bf16[1,512,1024]{2,1,0:T(8,128)(2,1)} %param.11) | copy-start | bytes 3145732
  7.2 132.7 %all-gather.2.cloned.1.call-start = ((), (), s32[]{:S(2)}) async-start(), calls=%async_computation.1 | async-start | bytes 11796480 | tf_op jit(solution)/shard_map/all_gather | solution.py:35
  10.3 264.2 %reduce-scatter.2.cloned.1.call-start = ((), (), s32[]{:S(2)}) async-start(), calls=%async_computation.2 | async-start | bytes 11796480 | tf_op jit(solution)/shard_map/reduce_scatter | solution.py:46
  21.8 5.4 %copy-start.1 = (f32[1,640,1024]{2,1,0:T(8,128)S(1)}, f32[1,640,1024]{2,1,0:T(8,128)}, u32[]{:S(2)}) copy-start(f32[1,640,1024]{2,1,0:T(8,128)} %param.13) | copy-start | bytes 7864324
  29.2 32.5 %collective-permute-start.4 = (bf16[640,1024]{1,0:T(8,128)(2,1)S(1)}, bf16[640,1024]{1,0:T(8,128)(2,1)}, u32[]{:S(2)}, u32[]{:S(2)}) collective-permute-start(bf16[640,1024]{1,0:T(8,128)(2,1)S(1)} %convert_element_type.54), channel_id=1, source_target_pairs={{0,32},{8,40},{16,48},{24,56},{32,0},{40,8},{48,16},{56,24},{64,96... | collective-permute-start | bytes 3932168 | tf_op jit(solution)/shard_map/cond/branch_2_fun/ppermute | solution.py:20
  33.5 56.2 %collective-permute-start.5 = (bf16[640,1024]{1,0:T(8,128)(2,1)S(1)}, bf16[640,1024]{1,0:T(8,128)(2,1)}, u32[]{:S(2)}, u32[]{:S(2)}) collective-permute-start(bf16[640,1024]{1,0:T(8,128)(2,1)S(1)} %convert_element_type.55), channel_id=1, source_target_pairs={{0,32},{8,40},{16,48},{24,56},{32,0},{40,8},{48,16},{56,24},{64,96... | collective-permute-start | bytes 3932168 | tf_op jit(solution)/shard_map/cond/branch_2_fun/ppermute | solution.py:20
  139.9 11.5 %copy-start.2 = (bf16[5120,1024]{1,0:T(8,128)(2,1)S(1)}, bf16[5120,1024]{1,0:T(8,128)(2,1)}, u32[]{:S(2)}) copy-start(bf16[5120,1024]{1,0:T(8,128)(2,1)} %all-gather.2.cloned.1.call-done) | copy-start | bytes 31457284
Sparse Core Ops, SparseCore 0:
  10.9 128.9 all-gather.1
  143.8 130.7 reduce-scatter.1
where the time goes:
time: 287 us
  waiting for transfers between devices  216 us (75%)
  matrix products  31 us (11%)
  other arithmetic  20.7 us (7%)
  between operations  14.7 us (5%)
  starting transfers between devices  4.3 us (1%)
    reduce_scatter x1, waiting for transfers between devices, on_device(): lax.psum_scatter((lax.dot_general(columns, cot_rows, (((0,), (0,)), ((),...  114 us
    ppermute x2, waiting for transfers between devices, partner(): return lax.ppermute(value, axis, pairs)  56.1 us
    all_gather x1, waiting for transfers between devices, on_device(): lax.all_gather(weights, 'tp', axis=0, tiled=True)  46 us
    dot_general x1, matrix products, on_device(): lax.dot_general(cot_rows, lax.all_gather(weights, 'tp', axis=0, tiled=Tru...  11.5 us
    dot_general x1, matrix products, on_device(): lax.dot_general(columns, cot_rows, (((0,), (0,)), ((), ())), preferred_el...  10.7 us
    broadcast_in_dim x2, other arithmetic, on_device(): return (keys[None], back[None], new_params[None], new_tracker[None])  10.1 us
    dot_general x1, matrix products, on_device(): jnp.dot(columns, lax.all_gather(weights, 'tp', axis=0, tiled=True), prefe...  8.83 us
  transfers between devices with their start and end apart: 4, of which 4 were waited for; matrix products, arithmetic and copies ran while one was open for 15% of the time, Pallas kernels for 0%

commit v1 on v0

v1 whole, which is shorter than its diff:
```python
import functools

import jax
import jax.numpy as jnp
from jax import lax
from jax.experimental import pallas as pl
from jax.experimental.pallas import tpu as pltpu
from jax.sharding import PartitionSpec as P

MESH = pl.DeviceIdType.MESH
Q = 4
NZ = 4
DEPTH = 3
F32, BF16 = jnp.float32, jnp.bfloat16
NT = (((1,), (1,)), ((), ()))
TN = (((0,), (0,)), ((), ()))


def kernel(
    level, scale,
    tok_h, cot_h, par_h, trk_h, old_h,
    keys_h, back_h, npar_h, ntrk_h,
    tok, cot, par, trk, old, w, part, rx, zh, zf, rt, mine, far, acc, kout, bout,
    load, store, bstore, xs, xr, ps, pr, ms, mr, fs, fr,
):
    rep, tp = lax.axis_index("rep"), lax.axis_index("tp")
    line, z = lax.div(tp, NZ), lax.rem(tp, NZ)
    rows = par.shape[0]
    wide = par.shape[1] // Q
    stride = 2**level
    bit = lax.rem(lax.div(rep, stride), 2)
    twin = (rep, lax.rem(tp + NZ, 2 * NZ))
    above = (rep, line * NZ + lax.rem(z + 1, NZ))
    below = (rep, line * NZ + lax.rem(z + NZ - 1, NZ))
    partner = (rep + stride * (1 - 2 * bit), tp)

    def col(q):
        return pl.ds(q * wide, wide)

    loads = [
        pltpu.make_async_copy(par_h.at[0, :, col(q)], par.at[:, col(q)], load.at[q]) for q in range(Q)
    ]
    loads.append(pltpu.make_async_copy(trk_h.at[0], trk, load.at[Q]))
    loads.append(pltpu.make_async_copy(cot_h.at[0], cot, load.at[Q + 1]))
    loads.append(pltpu.make_async_copy(tok_h.at[0], tok, load.at[Q + 2]))
    loads.append(pltpu.make_async_copy(old_h.at[0], old, load.at[Q + 3]))
    for c in loads:
        c.start()

    barrier = pltpu.get_barrier_semaphore()
    for other in (twin, above, below, partner):
        pl.semaphore_signal(barrier, 1, device_id=other, device_id_type=MESH)

    lo, hi = pl.ds(0, rows // 2), pl.ds(rows // 2, rows // 2)
    xl = [(("w", 4, q), w.at[0, q], w.at[4, q]) for q in range(Q)]
    order = [(2, 0), (2, 1), (2, 2), (1, 2), (3, 0), (1, 3), (3, 1), (1, 0), (3, 2), (1, 1), (3, 3)]
    order += [(0, q) for q in range(Q)]
    xl += [(("rx", j, q), part.at[4 + j, q], rx.at[j, q]) for j, q in order]
    pl_ = [(("w", 1, q), w.at[0, q], w.at[1, q]) for q in (0, 1, 2, 3)]
    pl_ += [(("rt", 0, 0), part.at[6, 3, lo], rt.at[0])]
    pl_ += [(("w", 2, q), w.at[1, q], w.at[2, q]) for q in (0, 1)]
    pl_ += [(("w", 5, q), w.at[4, q], w.at[5, q]) for q in (0, 1, 2, 3)]
    pl_ += [(("w", 6, q), w.at[5, q], w.at[6, q]) for q in (0, 1)]
    pl_ += [(("zh", 0, q), part.at[2, q], zh.at[0, q]) for q in (0, 1)]
    pl_ += [(("zf", 0, q), part.at[1, q], zf.at[0, q]) for q in (2, 3, 0, 1)]
    ml = [(("w", 3, q), w.at[0, q], w.at[3, q]) for q in (2, 3, 0, 1)]
    ml += [(("rt", 1, 0), part.at[6, 3, hi], rt.at[1])]
    ml += [(("w", 2, q), w.at[3, q], w.at[2, q]) for q in (2, 3)]
    ml += [(("w", 7, q), w.at[4, q], w.at[7, q]) for q in (2, 3, 0, 1)]
    ml += [(("w", 6, q), w.at[7, q], w.at[6, q]) for q in (2, 3)]
    ml += [(("zh", 1, q), part.at[2, q], zh.at[1, q - 2]) for q in (2, 3)]
    ml += [(("zf", 1, q), part.at[3, q], zf.at[1, q]) for q in (0, 1, 2, 3)]
    links = {}
    arrives = {}
    for name, items, dev, ssem, rsem in (
        ("x", xl, twin, xs, xr), ("p", pl_, above, ps, pr), ("m", ml, below, ms, mr),
    ):
        links[name] = []
        for i, (tag, src, dst) in enumerate(items):
            c = pltpu.make_async_remote_copy(
                src, dst, ssem.at[i], rsem.at[i], device_id=dev, device_id_type=MESH
            )
            links[name].append((tag, c))
            arrives[tag] = c
    pair = [
        pltpu.make_async_remote_copy(
            mine.at[i], far.at[i], fs.at[i], fr.at[i], device_id=partner, device_id_type=MESH
        )
        for i in range(2)
    ]
    seen = set()
    sent = {"x": 0, "p": 0, "m": 0}

    def need(*tag):
        if tag not in seen:
            seen.add(tag)
            arrives[tag].wait_recv()

    def widen(x):
        return x.astype(F32)

    def add_to(dst, *srcs):
        @pl.loop(0, dst.shape[0] // 80)
        def _(i):
            r = pl.ds(pl.multiple_of(i * 80, 80), 80)
            total = widen(dst[r, :])
            for s in srcs:
                total = total + widen(s[r, :])
            dst[r, :] = total.astype(BF16)

    def prepare(link, tag):
        kind, j, q = tag
        if kind == "w" and j in (5, 7):
            need("w", 4, q)
        if kind == "w" and j == 6:
            need("w", 5 if link == "p" else 7, q)
        if kind == "w" and j == 2:
            need("w", 1 if link == "p" else 3, q)
        if kind == "rx" and q == 3 and j in (1, 3):
            i = 0 if j == 1 else 1
            need("rt", i, 0)
            add_to(part.at[4 + j, 3, lo if i == 0 else hi], rt.at[i])
        if kind == "zh" and q != 3:
            need("rx", 2, q)
            add_to(part.at[2, q], rx.at[2, q])
        if kind == "zf":
            mid = 1 if link == "p" else 3
            need("rx", mid, q)
            more = [rx.at[mid, q]]
            if link == "p" and q in (0, 1):
                need("zh", 0, q)
                more.append(zh.at[0, q])
            if link == "m" and q in (2, 3):
                need("zh", 1, q)
                more.append(zh.at[1, q - 2])
            add_to(part.at[mid, q], *more)

    def issue(link, upto):
        while sent[link] < min(upto, len(links[link])):
            i = sent[link]
            tag, c = links[link][i]
            if i >= DEPTH:
                links[link][i - DEPTH][1].wait_send()
            prepare(link, tag)
            c.start()
            sent[link] = i + 1

    def cols_of(j):
        owner = lax.rem(line + lax.div(j, NZ), 2) * NZ + lax.rem(z + lax.rem(j, NZ), NZ)
        return pl.ds(pl.multiple_of(owner * rows, 128), rows)

    def partials(j):
        c = cols_of(j)

        @pl.loop(0, Q)
        def _(q):
            qc = pl.ds(pl.multiple_of(q * wide, 128), wide)
            g = lax.dot_general(tok[:, c], cot[:, qc], TN, preferred_element_type=F32)
            part[j, q] = (g * scale).astype(BF16)

    flight = [None, None]
    stores = []

    def use(slot):
        if slot:
            for q in range(Q):
                need("w", slot, q)
        j = (0, 3, 2, 1)[slot % 4] + 4 * (slot // 4)
        c = cols_of(j)
        b = len(stores) % 2
        if flight[b] is not None:
            flight[b].wait()

        @pl.loop(0, Q)
        def _(q):
            qc = pl.ds(pl.multiple_of(q * wide, 128), wide)
            t = jnp.dot(tok[:, c], w[slot, q], preferred_element_type=F32)
            if slot == 0:
                acc[:, qc] = t
            else:
                acc[:, qc] += t

        half = tok.shape[0] // 2

        @pl.loop(0, 2)
        def _(m):
            r = pl.ds(pl.multiple_of(m * half, half), half)
            t = lax.dot_general(cot[r, col(0)], w[slot, 0], NT, preferred_element_type=F32)
            for q in range(1, Q):
                t = t + lax.dot_general(cot[r, col(q)], w[slot, q], NT, preferred_element_type=F32)
            bout[b, r, :] = t.astype(BF16)

        flight[b] = pltpu.make_async_copy(bout.at[b], back_h.at[0, :, c], bstore.at[b])
        flight[b].start()
        stores.append(slot)

    for q in range(Q):
        loads[q].wait()
        w[0, q] = par[:, col(q)].astype(BF16)
        if q == 0:
            pl.semaphore_wait(barrier, 4)
            issue("x", 1)
            issue("p", 1)
    issue("m", 1)
    for n in range(2, DEPTH + 1):
        for link in ("x", "p", "m"):
            issue(link, n)

    loads[Q].wait()

    @pl.loop(0, rows // 32)
    def _(i):
        r = pl.ds(pl.multiple_of(i * 32, 32), 32)
        t = trk[r, :]
        mine[0, r, :] = (par[r, :] - 0.01 * t).astype(BF16)
        mine[1, r, :] = t.astype(BF16)

    pair[0].start()
    pair[1].start()
    loads[Q + 1].wait()
    loads[Q + 2].wait()
    loads[Q + 3].wait()

    @pl.loop(0, 8)
    def _(i):
        j = lax.rem(i + 6, 8)
        partials(j)

    def params_out():
        pair[0].wait_recv()

        @pl.loop(0, rows // 32)
        def _(i):
            r = pl.ds(pl.multiple_of(i * 32, 32), 32)
            half = par[r, :] - 0.01 * trk[r, :]
            par[r, :] = 0.5 * (half + widen(far[0, r, :]))

        c = pltpu.make_async_copy(par, npar_h.at[0], store.at[0])
        c.start()
        tail.append(c)

    def tracker_base():
        pair[1].wait_recv()

        @pl.loop(0, rows // 32)
        def _(i):
            r = pl.ds(pl.multiple_of(i * 32, 32), 32)
            trk[r, :] = 0.5 * (trk[r, :] + widen(far[1, r, :])) - old[r, :]

    def keys_out():
        @pl.loop(0, 8)
        def _(i):
            n = tok.shape[0] // 8
            r = pl.ds(pl.multiple_of(i * n, n), n)
            kout[r, :] = acc[r, :].astype(BF16)

        c = pltpu.make_async_copy(kout, keys_h.at[0], store.at[1])
        c.start()
        tail.append(c)

    tail = []
    work = {
        3: [lambda: use(0)],
        5: [lambda: use(1)],
        6: [lambda: use(3)],
        7: [lambda: use(4)],
        9: [lambda: use(2)],
        10: [params_out],
        11: [tracker_base],
        12: [lambda: use(5)],
        13: [lambda: use(7)],
        15: [lambda: use(6)],
        16: [keys_out],
    }
    longest = max(len(v) for v in links.values())
    for t in range(3, longest):
        for link in ("x", "p", "m"):
            issue(link, t + 1)
        for job in work.get(t, ()):
            job()

    for q in range(Q):
        need("zf", 0, q)
        need("zf", 1, q)
        need("rx", 0, q)

        @pl.loop(0, rows // 80)
        def _(i):
            r = pl.ds(pl.multiple_of(i * 80, 80), 80)
            g = widen(part[0, q, r, :]) + widen(rx[0, q, r, :])
            g = g + widen(zf[0, q, r, :]) + widen(zf[1, q, r, :])
            trk[r, col(q)] += g

        c = pltpu.make_async_copy(trk.at[:, col(q)], ntrk_h.at[0, :, col(q)], store.at[2 + q])
        c.start()
        tail.append(c)

    for name, items in links.items():
        for tag, c in items:
            if tag not in seen:
                seen.add(tag)
                c.wait_recv()
        for tag, c in items[max(0, len(items) - DEPTH):]:
            c.wait_send()
    for c in pair:
        c.wait_send()
    for c in flight + tail:
        c.wait()


def call(level, tokens, cotangent, params, tracker, grad_old):
    _, toks, d = tokens.shape
    _, rows, kv = params.shape
    wide = kv // Q
    scale = 1.0 / float(toks * 2 * NZ) ** 0.5
    sem = pltpu.SemaphoreType.DMA
    any_ = pl.BlockSpec(memory_space=pl.ANY)
    return pl.pallas_call(
        functools.partial(kernel, level, scale),
        out_shape=(
            jax.ShapeDtypeStruct(cotangent.shape, BF16),
            jax.ShapeDtypeStruct(tokens.shape, BF16),
            jax.ShapeDtypeStruct(params.shape, F32),
            jax.ShapeDtypeStruct(params.shape, F32),
        ),
        in_specs=[any_] * 5,
        out_specs=(any_,) * 4,
        scratch_shapes=[
            pltpu.VMEM((toks, d), BF16),
            pltpu.VMEM((toks, kv), BF16),
            pltpu.VMEM((rows, kv), F32),
            pltpu.VMEM((rows, kv), F32),
            pltpu.VMEM((rows, kv), F32),
            pltpu.VMEM((8, Q, rows, wide), BF16),
            pltpu.VMEM((8, Q, rows, wide), BF16),
            pltpu.VMEM((NZ, Q, rows, wide), BF16),
            pltpu.VMEM((2, 2, rows, wide), BF16),
            pltpu.VMEM((2, Q, rows, wide), BF16),
            pltpu.VMEM((2, rows // 2, wide), BF16),
            pltpu.VMEM((2, rows, kv), BF16),
            pltpu.VMEM((2, rows, kv), BF16),
            pltpu.VMEM((toks, kv), F32),
            pltpu.VMEM((toks, kv), BF16),
            pltpu.VMEM((2, toks, rows), BF16),
            sem((Q + 4,)), sem((Q + 2,)), sem((2,)),
            sem((19,)), sem((19,)), sem((19,)), sem((19,)), sem((19,)), sem((19,)), sem((2,)), sem((2,)),
        ],
        compiler_params=pltpu.CompilerParams(
            collective_id=level, has_side_effects=True, vmem_limit_bytes=60 << 20
        ),
        cost_estimate=pl.CostEstimate(
            flops=6 * toks * d * kv, bytes_accessed=26 << 20, transcendentals=0
        ),
        name=f"train_step_{level}",
    )(tokens, cotangent, params, tracker, grad_old)


def on_device(tokens, cotangent, params, tracker, grad_old, step):
    branches = [functools.partial(call, level) for level in range(3)]
    return lax.switch(
        jnp.clip(step[0], 0, 2), branches, tokens, cotangent, params, tracker, grad_old
    )


def solution(mesh):
    rows = P("rep", "tp", None)
    return jax.shard_map(
        on_device,
        mesh=mesh,
        in_specs=(rows,) * 5 + (P(),),
        out_specs=(rows,) * 4,
        check_vma=False,
    )
```

time: 287 us -> 157 us (0.55)
  waiting for transfers between devices: 216 us -> 0 us
  Pallas kernels: 0 us -> 143 us
  matrix products: 31 us -> 0 us
  other arithmetic: 20.7 us -> 0 us
  between operations: 14.7 us -> 1.29 us
  local copies, waits for them, and re-layouts: 0.02 us -> 11.6 us
  starting transfers between devices: 4.3 us -> 0 us
    pallas_call x0 -> x1, Pallas kernels: none -> 143 us  [call(): pl.pallas_call(functools.partial(kernel, level, scale), out_shape=(jax.Sh...]
    reduce_scatter x1 -> x0, waiting for transfers between devices: 114 us -> none  [on_device(): lax.psum_scatter((lax.dot_general(columns, cot_rows, (((0,), (0,)), ((),...]
    ppermute x2 -> x0, waiting for transfers between devices: 56.1 us -> none  [partner(): return lax.ppermute(value, axis, pairs)]
    all_gather x1 -> x0, waiting for transfers between devices: 46 us -> none  [on_device(): lax.all_gather(weights, 'tp', axis=0, tiled=True)]
    dot_general x3 -> x0, matrix products: 31 us -> none  [the longest x1 11.5 us: on_device(): lax.dot_general(cot_rows, lax.all_gather(weights, 'tp', axis=0, tiled=Tru...]
    unnamed x6, local copies, waits for them, and re-layouts: 0.02 us -> 11.6 us
    broadcast_in_dim x2 -> x0, other arithmetic: 10.1 us -> none  [on_device(): return (keys[None], back[None], new_params[None], new_tracker[None])]
    sub x1 -> x0, other arithmetic: 5.42 us -> none  [on_device(): half = params[0] - 0.01 * tracker[0]]
  transfers between devices with their start and end apart: 4 -> 0, of which waited for: 4 -> 0; matrix products, arithmetic and copies ran while one was open for 15% -> 0% of each run, Pallas kernels for 0% -> 0%
where the time goes in v1:
time: 157 us; the launch traced here: 156 us
  Pallas kernels  143 us (91%)
  local copies, waits for them, and re-layouts  11.6 us (7%)
    pallas_call x1, Pallas kernels, call(): pl.pallas_call(functools.partial(kernel, level, scale), out_shape=(jax.Sh...  143 us
    unnamed x6, local copies, waits for them, and re-layouts  11.6 us

profile of v1, /device:TPU:1, one launch (start us, length us, event | category | flops | bytes accessed | tf_op | source)
XLA Modules:
  0.0 156.5 jit_solution(7984640218601476361)
XLA Ops:
  1.3 143.5 %conditional.1 = ((bf16[1,512,1024]{2,1,0:T(8,128)(2,1)}, bf16[1,512,5120]{2,1,0:T(8,128)(2,1)}, f32[1,640,1024]{2,1,0:T(8,128)S(1)}, f32[1,640,1024]{2,1,0:T(8,128)})) conditional(s32[]{:T(128)} %bitcast, (bf16[1,512,5120]{2,1,0:T(8,128)(2,1)}, bf16[1,512,1024]{2,1,0:T(8,128)(2,1)}, f32[1,640,1024]{2,1,0:T(8,128)}, ...), branch_computations={%region_0.1_spmd, %region_1.2_spmd, %region_2.3_spmd} | conditional | flops 16106127360 | bytes 27262984 | solution.py:360
  1.3 143.3 %train_step_0.1 = (bf16[1,512,1024]{2,1,0:T(8,128)(2,1)}, bf16[1,512,5120]{2,1,0:T(8,128)(2,1)}, f32[1,640,1024]{2,1,0:T(8,128)S(1)}, f32[1,640,1024]{2,1,0:T(8,128)}) custom-call(bf16[1,512,5120]{2,1,0:T(8,128)(2,1)} %get-tuple-element.30.tok_h, bf16[1,512,1024]{2,1,0:T(8,128)(2,1)} %get-tuple-element.31.cot_h, f32[1,640,1024]{2,1,0:T(8,128)} %get-tuple-element.32.par_h, ...), custom_call_target="tpu_custom_call" | custom-call | flops 16106127360 | bytes 27262976 | tf_op jit(solution)/shard_map/cond/branch_0_fun/train_step_0/pallas_call | solution.py:318
  144.8 2.3 %copy.39 = bf16[1,512,1024]{2,1,0:T(8,128)(2,1)} copy(bf16[1,512,1024]{2,1,0:T(8,128)(2,1)} %get-tuple-element.81) | data formatting | bytes 2097152
  147.1 5.2 %copy.40 = bf16[1,512,5120]{2,1,0:T(8,128)(2,1)} copy(bf16[1,512,5120]{2,1,0:T(8,128)(2,1)} %get-tuple-element.82) | data formatting | bytes 10485760
  152.3 0.0 copy-start
  152.3 1.5 copy.41
  153.8 1.2 copy-done
  155.0 1.5 copy.42
Async XLA Ops:
  152.3 2.7 %copy-start = (f32[1,640,1024]{2,1,0:T(8,128)S(1)}, f32[1,640,1024]{2,1,0:T(8,128)}, u32[]{:S(2)}) copy-start(f32[1,640,1024]{2,1,0:T(8,128)} %get-tuple-element.84) | copy-start | bytes 7864324

commit v2 on v0

v2 whole, which is shorter than its diff:
```python
import functools

import jax
import jax.numpy as jnp
from jax import lax
from jax.experimental import pallas as pl
from jax.experimental.pallas import tpu as pltpu
from jax.sharding import PartitionSpec as P

MESH = pl.DeviceIdType.MESH
Q = 4
NZ = 4
DEPTH = 2
F32, BF16 = jnp.float32, jnp.bfloat16
NT = (((1,), (1,)), ((), ()))
TN = (((0,), (0,)), ((), ()))


def kernel(
    level, scale,
    tok_h, cot_h, par_h, trk_h, old_h,
    keys, back, par, trk,
    tok, cot, old, w, part, tokb, cotb, zh, zf, mine, far, acc,
    load, xs, xr, ps, pr, ms, mr, fs, fr,
):
    rep, tp = lax.axis_index("rep"), lax.axis_index("tp")
    line, z = lax.div(tp, NZ), lax.rem(tp, NZ)
    toks = tok.shape[0]
    rows, kv = par.shape
    wide = kv // Q
    stride = 2**level
    bit = lax.rem(lax.div(rep, stride), 2)
    twin = (rep, lax.rem(tp + NZ, 2 * NZ))
    above = (rep, line * NZ + lax.rem(z + 1, NZ))
    below = (rep, line * NZ + lax.rem(z + NZ - 1, NZ))
    partner = (rep + stride * (1 - 2 * bit), tp)
    cut = rows * 2 // 5 // 128 * 128
    spans = ((0, cut), (cut, rows - cut))

    def col(q):
        return pl.ds(q * wide, wide)

    def cols_of(j, at=0, n=None, other=0):
        owner = lax.rem(line + other, 2) * NZ + lax.rem(z + j, NZ)
        return pl.ds(pl.multiple_of(owner * rows + at, 128), rows if n is None else n)

    loads = {"cot": pltpu.make_async_copy(cot_h.at[0], cot, load.at[0])}
    for q in range(Q):
        loads[q] = pltpu.make_async_copy(par_h.at[0, :, col(q)], par.at[:, col(q)], load.at[1 + q])
    loads["tok"] = pltpu.make_async_copy(tok_h.at[0], tok, load.at[Q + 1])
    loads["trk"] = pltpu.make_async_copy(trk_h.at[0], trk, load.at[Q + 2])
    loads["old"] = pltpu.make_async_copy(old_h.at[0], old, load.at[Q + 3])
    for c in loads.values():
        c.start()

    barrier = pltpu.get_barrier_semaphore()
    for other in (twin, above, below, partner):
        pl.semaphore_signal(barrier, 1, device_id=other, device_id_type=MESH)

    def shard(slot, q, src):
        return (("w", slot, q), 1.0, w.at[src, q], w.at[slot, q])

    def factor(j, i):
        at, n = spans[i]
        src = tok.at[:, cols_of(j, at, n, other=1)]
        return (("t", j, i), 2.0 * n / rows, src, tokb.at[j, :, pl.ds(at, n)])

    def finished(j, i):
        n = rows // 5
        r = pl.ds(i * n, n)
        k = 0 if j == 1 else 1
        return (("zf", k, i), 0.8, part.at[j - 1, r], zf.at[k, r])

    def passed(k, i):
        n = rows // 4
        return (
            ("zh", k, i), 1.0, part.at[1, pl.ds((2 * k + i) * n, n)], zh.at[k, pl.ds(i * n, n)],
        )

    half = toks // 2
    xl = [(("c", 0, i), 1.6, cot.at[pl.ds(i * half, half)], cotb.at[pl.ds(i * half, half)]) for i in (0, 1)]
    xl += [factor(2, 0), factor(2, 1)]
    xl += [shard(4, q, 0) for q in (0, 3, 1, 2)]
    xl += [factor(1, 0), factor(3, 0), factor(1, 1), factor(3, 1)]
    xl += [shard(6, q, 2) for q in (1, 2)]
    xl += [factor(0, 0), factor(0, 1)]
    up = [shard(1, q, 0) for q in (0, 1, 2, 3)]
    up += [shard(2, q, 1) for q in (0, 1)]
    up += [passed(0, 0), passed(0, 1)]
    up += [shard(5, q, 4) for q in (0, 3, 1, 2)]
    up += [shard(6, 0, 5)]
    up += [finished(1, i) for i in range(5)]
    down = [shard(3, q, 0) for q in (2, 3, 0, 1)]
    down += [shard(2, q, 3) for q in (2, 3)]
    down += [passed(1, 0), passed(1, 1)]
    down += [shard(7, q, 4) for q in (3, 0, 1, 2)]
    down += [shard(6, 3, 7)]
    down += [finished(3, i) for i in range(5)]
    made = {("p", "zh", False): 5.3, ("m", "zh", False): 5.3}
    made |= {("p", "zf", False): 10.2, ("m", "zf", False): 11.0}
    made |= {("p", "zf", True): 12.2, ("m", "zf", True): 13.4}
    links, arrives, program = {}, {}, []
    for name, items, dev, ssem, rsem in (
        ("x", xl, twin, xs, xr), ("p", up, above, ps, pr), ("m", down, below, ms, mr),
    ):
        links[name] = []
        ends = []
        for i, (tag, ticks, src, dst) in enumerate(items):
            c = pltpu.make_async_remote_copy(
                src, dst, ssem.at[i], rsem.at[i], device_id=dev, device_id_type=MESH
            )
            links[name].append((tag, c))
            arrives[tag] = c
            free = ends[i - DEPTH] if i >= DEPTH else 0.0
            program.append((max(free, made.get((name, tag[0], tag[2] > 1), 0.0)), name, i))
            ends.append((ends[-1] if ends else 0.0) + ticks)
    pair = [
        pltpu.make_async_remote_copy(
            mine.at[i], far.at[i], fs.at[i], fr.at[i], device_id=partner, device_id_type=MESH
        )
        for i in range(2)
    ]
    seen, ready = set(), set()

    def need(*tag):
        if tag not in seen:
            seen.add(tag)
            arrives[tag].wait_recv()

    def widen(x):
        return x.astype(F32)

    def add_rows(k, at, n):
        @pl.loop(0, n // 64)
        def _(i):
            r = pl.ds(pl.multiple_of(at + i * 64, 64), 64)
            s = pl.ds(pl.multiple_of(at + i * 64 - k * (rows // 2), 64), 64)
            part[2 * k, r, :] = (widen(part[2 * k, r, :]) + widen(zh[k, s, :])).astype(BF16)

    def prepare(link, tag):
        kind, j, q = tag
        if kind == "w" and j in (5, 7):
            need("w", 4, q)
        if kind == "w" and j == 6:
            need("w", {"x": 2, "p": 5, "m": 7}[link], q)
        if kind == "w" and j == 2:
            need("w", 1 if link == "p" else 3, q)
        if kind == "zh":
            assert {(2, 0), (2, 1)} <= ready
        if kind == "zf":
            assert (1 if link == "p" else 3, 0 if q < 2 else 1) in ready

    def issue(link, i):
        tag, c = links[link][i]
        if i >= DEPTH:
            links[link][i - DEPTH][1].wait_send()
        prepare(link, tag)
        c.start()

    def product(j, i, q, own=True, twins=True):
        at, n = spans[i]
        qc = pl.ds(pl.multiple_of(q * wide, 128), wide)
        g = 0.0
        if own:
            g = g + lax.dot_general(tok[:, cols_of(j, at, n)], cot[:, qc], TN, preferred_element_type=F32)
        if twins:
            g = g + lax.dot_general(
                tokb[j, :, pl.ds(at, n)], cotb[:, qc], TN, preferred_element_type=F32
            )
        return g * scale, pl.ds(at, n), qc

    def sums(j, i):
        need("c", 0, 0)
        need("c", 0, 1)
        need("t", j, i)

        @pl.loop(0, Q)
        def _(q):
            g, r, qc = product(j, i, q)
            part[j - 1, r, qc] = g.astype(BF16)

        if j != 2:
            k = 0 if j == 1 else 1
            need("zh", k, 0)
            need("zh", k, 1)
            at, n = spans[i]
            first, last = max(at, k * (rows // 2)), min(at + n, (k + 1) * (rows // 2))
            if last > first:
                add_rows(k, first, last - first)
        ready.add((j, i))

    def own_sum(i, own, twins):
        assert "base" in ready
        if twins:
            need("t", 0, i)

        @pl.loop(0, Q)
        def _(q):
            g, r, qc = product(0, i, q, own, twins)
            trk[r, qc] += g

    def add_finished(i):
        assert "base" in ready
        need("zf", 0, i)
        need("zf", 1, i)
        n = rows // 5

        @pl.loop(0, n // 32)
        def _(m):
            r = pl.ds(pl.multiple_of(i * n + m * 32, 32), 32)
            trk[r, :] += widen(zf[0, r, :]) + widen(zf[1, r, :])

    def use(slot):
        if slot:
            for q in range(Q):
                need("w", slot, q)
        c = cols_of((0, 3, 2, 1)[slot % 4], other=slot // 4)

        @pl.loop(0, Q)
        def _(q):
            qc = pl.ds(pl.multiple_of(q * wide, 128), wide)
            t = jnp.dot(tok[:, c], w[slot, q], preferred_element_type=F32)
            if slot == 0:
                acc[:, qc] = t
            else:
                acc[:, qc] += t

        @pl.loop(0, 2)
        def _(m):
            r = pl.ds(pl.multiple_of(m * half, half), half)
            t = lax.dot_general(cot[r, col(0)], w[slot, 0], NT, preferred_element_type=F32)
            for q in range(1, Q):
                t = t + lax.dot_general(cot[r, col(q)], w[slot, q], NT, preferred_element_type=F32)
            back[r, c] = t.astype(BF16)

    def send_pair():
        loads["trk"].wait()

        @pl.loop(0, rows // 32)
        def _(i):
            r = pl.ds(pl.multiple_of(i * 32, 32), 32)
            t = trk[r, :]
            mine[0, r, :] = (par[r, :] - 0.01 * t).astype(BF16)
            mine[1, r, :] = t.astype(BF16)

        pair[0].start()
        pair[1].start()

    def average():
        loads["old"].wait()
        pair[0].wait_recv()
        pair[1].wait_recv()

        @pl.loop(0, rows // 32)
        def _(i):
            r = pl.ds(pl.multiple_of(i * 32, 32), 32)
            t = trk[r, :]
            par[r, :] = 0.5 * ((par[r, :] - 0.01 * t) + widen(far[0, r, :]))
            trk[r, :] = 0.5 * (t + widen(far[1, r, :])) - old[r, :]

        ready.add("base")

    def keys_out():
        @pl.loop(0, 8)
        def _(i):
            n = toks // 8
            r = pl.ds(pl.multiple_of(i * n, n), n)
            keys[r, :] = acc[r, :].astype(BF16)

    loads["cot"].wait()
    pl.semaphore_wait(barrier, 4)
    issue("x", 0)
    for n, q in enumerate((0, 2, 1, 3)):
        loads[q].wait()
        w[0, q] = par[:, col(q)].astype(BF16)
        issue("pmpm"[n], n // 2)
    for i in range(1, DEPTH):
        issue("x", i)
    loads["tok"].wait()

    jobs = [
        (0.1, send_pair),
        (0.6, lambda: use(0)),
        (4.2, lambda: use(1)),
        (4.6, lambda: use(3)),
        (5.2, lambda: (sums(2, 0), sums(2, 1))),
        (6.7, lambda: use(2)),
        (9.3, average),
        (9.4, lambda: use(4)),
        (9.6, lambda: (own_sum(0, True, False), own_sum(1, True, False))),
        (10.1, lambda: sums(1, 0)),
        (10.9, lambda: sums(3, 0)),
        (12.1, lambda: sums(1, 1)),
        (12.3, lambda: use(5)),
        (13.3, lambda: sums(3, 1)),
        (13.4, lambda: use(7)),
        (15.3, lambda: (use(6), keys_out())),
        (16.1, lambda: own_sum(0, False, True)),
        (16.3, lambda: (add_finished(0), add_finished(1), add_finished(2))),
    ]
    started = {"x": DEPTH, "p": 2, "m": 2}
    order = [(key, 0, name, i) for key, name, i in program if i >= started[name]]
    order += [(key, 1, "", job) for key, job in jobs]
    for key, kind, name, what in sorted(order, key=lambda e: e[:3]):
        if kind:
            what()
        else:
            issue(name, what)
    own_sum(1, False, True)
    add_finished(3)
    add_finished(4)

    for name, items in links.items():
        for tag, c in items:
            if tag not in seen:
                seen.add(tag)
                c.wait_recv()
        for tag, c in items[-DEPTH:]:
            c.wait_send()
    for c in pair:
        c.wait_send()


def write_out(keys, back, par, trk, keys_h, back_h, par_h, trk_h, done):
    copies = []
    for src, dst in ((back, back_h), (par, par_h), (trk, trk_h), (keys, keys_h)):
        n = src.shape[0] // 4
        for i in range(4):
            r = pl.ds(i * n, n)
            copies.append(pltpu.make_async_copy(src.at[r], dst.at[0, r], done.at[len(copies)]))
    for c in copies:
        c.start()
    for c in copies:
        c.wait()


def call(level, tokens, cotangent, params, tracker, grad_old):
    _, toks, d = tokens.shape
    _, rows, kv = params.shape
    wide = kv // Q
    scale = 1.0 / float(toks * 2 * NZ) ** 0.5
    sem = pltpu.SemaphoreType.DMA
    hbm = pl.BlockSpec(memory_space=pltpu.HBM)
    vmem = pl.BlockSpec(memory_space=pltpu.VMEM)
    results = pl.pallas_call(
        functools.partial(kernel, level, scale),
        out_shape=(
            pltpu.VMEM((toks, kv), BF16),
            pltpu.VMEM((toks, d), BF16),
            pltpu.VMEM((rows, kv), F32),
            pltpu.VMEM((rows, kv), F32),
        ),
        in_specs=[hbm] * 5,
        out_specs=(vmem,) * 4,
        scratch_shapes=[
            pltpu.VMEM((toks, d), BF16),
            pltpu.VMEM((toks, kv), BF16),
            pltpu.VMEM((rows, kv), F32),
            pltpu.VMEM((8, Q, rows, wide), BF16),
            pltpu.VMEM((3, rows, kv), BF16),
            pltpu.VMEM((NZ, toks, rows), BF16),
            pltpu.VMEM((toks, kv), BF16),
            pltpu.VMEM((2, rows // 2, kv), BF16),
            pltpu.VMEM((2, rows, kv), BF16),
            pltpu.VMEM((2, rows, kv), BF16),
            pltpu.VMEM((2, rows, kv), BF16),
            pltpu.VMEM((toks, kv), F32),
            sem((Q + 4,)),
            sem((16,)), sem((16,)), sem((18,)), sem((18,)), sem((18,)), sem((18,)), sem((2,)), sem((2,)),
        ],
        compiler_params=pltpu.CompilerParams(
            collective_id=level, has_side_effects=True, vmem_limit_bytes=50 << 20
        ),
        cost_estimate=pl.CostEstimate(
            flops=6 * toks * d * kv, bytes_accessed=14 << 20, transcendentals=0
        ),
        name=f"train_step_{level}",
    )(tokens, cotangent, params, tracker, grad_old)
    return pl.pallas_call(
        write_out,
        out_shape=(
            jax.ShapeDtypeStruct(cotangent.shape, BF16),
            jax.ShapeDtypeStruct(tokens.shape, BF16),
            jax.ShapeDtypeStruct(params.shape, F32),
            jax.ShapeDtypeStruct(params.shape, F32),
        ),
        in_specs=[vmem] * 4,
        out_specs=(hbm,) * 4,
        scratch_shapes=[sem((16,))],
        compiler_params=pltpu.CompilerParams(vmem_limit_bytes=1 << 20),
        name="write_out",
    )(*[pltpu.with_memory_space_constraint(r, pltpu.VMEM) for r in results])


def on_device(tokens, cotangent, params, tracker, grad_old, step):
    branches = [functools.partial(call, level) for level in range(3)]
    return lax.switch(
        jnp.clip(step[0], 0, 2), branches, tokens, cotangent, params, tracker, grad_old
    )


def solution(mesh):
    rows = P("rep", "tp", None)
    return jax.shard_map(
        on_device,
        mesh=mesh,
        in_specs=(rows,) * 5 + (P(),),
        out_specs=(rows,) * 4,
        check_vma=False,
    )
```

time: 287 us -> 137 us (0.48)
  waiting for transfers between devices: 216 us -> 0 us
  Pallas kernels: 0 us -> 135 us
  matrix products: 31 us -> 0 us
  other arithmetic: 20.7 us -> 0 us
  between operations: 14.7 us -> 1.48 us
  starting transfers between devices: 4.3 us -> 0 us
    pallas_call x0 -> x2, Pallas kernels: none -> 135 us  [the longest x1 131 us: call(): pl.pallas_call(functools.partial(kernel, level, scale), out_shape=(pltpu....]
    reduce_scatter x1 -> x0, waiting for transfers between devices: 114 us -> none  [on_device(): lax.psum_scatter((lax.dot_general(columns, cot_rows, (((0,), (0,)), ((),...]
    ppermute x2 -> x0, waiting for transfers between devices: 56.1 us -> none  [partner(): return lax.ppermute(value, axis, pairs)]
    all_gather x1 -> x0, waiting for transfers between devices: 46 us -> none  [on_device(): lax.all_gather(weights, 'tp', axis=0, tiled=True)]
    dot_general x3 -> x0, matrix products: 31 us -> none  [the longest x1 11.5 us: on_device(): lax.dot_general(cot_rows, lax.all_gather(weights, 'tp', axis=0, tiled=Tru...]
    broadcast_in_dim x2 -> x0, other arithmetic: 10.1 us -> none  [on_device(): return (keys[None], back[None], new_params[None], new_tracker[None])]
    sub x1 -> x0, other arithmetic: 5.42 us -> none  [on_device(): half = params[0] - 0.01 * tracker[0]]
    convert_element_type x3 -> x0, other arithmetic: 5.2 us -> none  [the longest x1 3.08 us: on_device(): weights = params[0].astype(jnp.bfloat16)]
  transfers between devices with their start and end apart: 4 -> 0, of which waited for: 4 -> 0; matrix products, arithmetic and copies ran while one was open for 15% -> 0% of each run, Pallas kernels for 0% -> 0%
where the time goes in v2:
time: 137 us
  Pallas kernels  135 us (99%)
  between operations  1.48 us (1%)
    pallas_call x1, Pallas kernels, call(): pl.pallas_call(functools.partial(kernel, level, scale), out_shape=(pltpu....  131 us
    pallas_call x1, Pallas kernels, call(): pl.pallas_call(write_out, out_shape=(jax.ShapeDtypeStruct(cotangent.shape...  4.38 us

profile of v2, /device:TPU:1, one launch (start us, length us, event | category | flops | bytes accessed | tf_op | source)
XLA Modules:
  0.0 137.0 jit_solution(1784470268366232560)
XLA Ops:
  1.3 135.5 %conditional.1 = ((bf16[1,512,1024]{2,1,0:T(8,128)(2,1)}, bf16[1,512,5120]{2,1,0:T(8,128)(2,1)}, f32[1,640,1024]{2,1,0:T(8,128)}, f32[1,640,1024]{2,1,0:T(8,128)})) conditional(s32[]{:T(128)} %bitcast, (bf16[1,512,5120]{2,1,0:T(8,128)(2,1)}, bf16[1,512,1024]{2,1,0:T(8,128)(2,1)}, f32[1,640,1024]{2,1,0:T(8,128)}, ...), branch_computations={%region_0.1_spmd, %region_1.2_spmd, %region_2.3_spmd} | conditional | flops 16106127360 | bytes 14680072 | solution.py:397
  1.3 130.8 %train_step_0.1 = (bf16[512,1024]{1,0:T(8,128)(2,1)S(1)}, bf16[512,5120]{1,0:T(8,128)(2,1)S(1)}, f32[640,1024]{1,0:T(8,128)S(1)}, f32[640,1024]{1,0:T(8,128)S(1)}) custom-call(bf16[1,512,5120]{2,1,0:T(8,128)(2,1)} %get-tuple-element.30.tok_h, bf16[1,512,1024]{2,1,0:T(8,128)(2,1)} %get-tuple-element.31.cot_h, f32[1,640,1024]{2,1,0:T(8,128)} %get-tuple-element.32.par_h, ...), custom_call_target="tpu_custom_call" | custom-call | flops 16106127360 | bytes 14680064 | tf_op jit(solution)/shard_map/cond/branch_0_fun/train_step_0/pallas_call | solution.py:345
  132.1 4.4 %write_out.3 = (bf16[1,512,1024]{2,1,0:T(8,128)(2,1)}, bf16[1,512,5120]{2,1,0:T(8,128)(2,1)}, f32[1,640,1024]{2,1,0:T(8,128)}, f32[1,640,1024]{2,1,0:T(8,128)}) custom-call(bf16[512,1024]{1,0:T(8,128)(2,1)S(1)} %get-tuple-element.35.keys, bf16[512,5120]{1,0:T(8,128)(2,1)S(1)} %get-tuple-element.36.back, f32[640,1024]{1,0:T(8,128)S(1)} %get-tuple-element.37.par, ...), custom_call_target="tpu_custom_call" | custom-call | tf_op jit(solution)/shard_map/cond/branch_0_fun/write_out/pallas_call | solution.py:379

commit v3 on v2

v3 whole, which is shorter than its diff:
```python
import functools

import jax
import jax.numpy as jnp
from jax import lax
from jax.experimental import pallas as pl
from jax.experimental.pallas import tpu as pltpu
from jax.sharding import PartitionSpec as P

MESH = pl.DeviceIdType.MESH
Q = 4
NZ = 4
DEPTH = 3
F32, BF16 = jnp.float32, jnp.bfloat16
NT = (((1,), (1,)), ((), ()))
TN = (((0,), (0,)), ((), ()))


def kernel(
    level, scale,
    tok_h, cot_h, par_h, trk_h, old_h,
    keys, back, par, trk,
    tok, cot, old, w, part, tokp, cotp, rx, zf, mine, far, acc, accp, backp, keysp, keysi,
    load, xs, xr, ps, pr, ms, mr, fs, fr,
):
    rep, tp = lax.axis_index("rep"), lax.axis_index("tp")
    line, z = lax.div(tp, NZ), lax.rem(tp, NZ)
    toks = tok.shape[0]
    rows, kv = par.shape
    wide = kv // Q
    stride = 2**level
    bit = lax.rem(lax.div(rep, stride), 2)
    step = 1 - 2 * lax.rem(z + rep, 2)
    zp, zi = lax.rem(z + step + NZ, NZ), lax.rem(z - step + NZ, NZ)
    twin = (rep, lax.rem(tp + NZ, 2 * NZ))
    pal = (rep, line * NZ + zp)
    near = (rep, line * NZ + zi)
    partner = (rep + stride * (1 - 2 * bit), tp)

    def col(q):
        return pl.ds(q * wide, wide)

    def cols_of(slot, pals=False):
        a, b = (zp, lax.rem(z + 2, NZ)) if pals else (z, zi)
        owner = lax.rem(line + slot // 2, 2) * NZ + (b if slot % 2 else a)
        return pl.ds(pl.multiple_of(owner * rows, 128), rows)

    barrier = pltpu.get_barrier_semaphore()
    for other in (twin, pal, near, partner):
        pl.semaphore_signal(barrier, 1, device_id=other, device_id_type=MESH)
    loads = {"cot": pltpu.make_async_copy(cot_h.at[0], cot, load.at[0])}
    for q in range(Q):
        loads[q] = pltpu.make_async_copy(par_h.at[0, :, col(q)], par.at[:, col(q)], load.at[1 + q])
    loads["tok"] = pltpu.make_async_copy(tok_h.at[0], tok, load.at[Q + 1])
    loads["trk"] = pltpu.make_async_copy(trk_h.at[0], trk, load.at[Q + 2])
    loads["old"] = pltpu.make_async_copy(old_h.at[0], old, load.at[Q + 3])
    for c in loads.values():
        c.start()

    half, n4 = toks // 2, rows // 4
    cut = rows // 2
    lo, hi = pl.ds(0, cut), pl.ds(cut, rows - cut)

    def quarter(i):
        return pl.ds(i * n4, n4)

    def halves(i):
        return pl.ds(i * half, half)

    xl = [(("w", 2, q), 0.0, w.at[0, q], w.at[2, q]) for q in range(Q)]
    xl += [(("w", 3, q), q + 1.2, w.at[1, q], w.at[3, q]) for q in range(3)]
    xl += [(("w", 3, 3), 4.2, w.at[1, 3, lo], w.at[3, 3, lo])]
    xl += [(("rx", 1, i), 5.2, part.at[2, quarter(i)], rx.at[1, quarter(i)]) for i in range(4)]
    xl += [(("rx", 0, i), 6.1, part.at[1, quarter(i)], rx.at[0, quarter(i)]) for i in range(4)]
    xend = [1, 2, 3, 4, 5, 6, 7, 7.5, 8.5, 9.5, 10.5, 11.5, 12.5, 13.5, 14.5, 15.5]
    pp = [(("c", 0, i), 0.0, cot.at[halves(i)], cotp.at[halves(i)]) for i in (0, 1)]
    pp += [(("t", s, 0), 0.1, tok.at[:, cols_of(s, True)], tokp.at[s]) for s in (3, 2, 1, 0)]
    pp += [(("b", s, 0), t, backp.at[s], back.at[:, cols_of(s)]) for s, t in ((0, 3.7), (1, 4.7), (2, 4.8))]
    pp += [(("k", 0, 0), 9.0, keysp, keysi)]
    pp += [(("b", 3, 0), 8.5, backp.at[3], back.at[:, cols_of(3)])]
    pend = [1.6, 3.2, 4.6, 5.6, 6.6, 7.6, 8.6, 9.6, 10.6, 13.4, 15.4]
    ml = [(("w", 1, q), 0.0, w.at[0, q], w.at[1, q]) for q in range(Q)]
    ml += [(("v", 3, 3), 4.3, w.at[2, 3, hi], w.at[3, 3, hi])]
    ml += [(("zf", 0, i), 8.7 + i, part.at[0, quarter(i)], zf.at[quarter(i)]) for i in range(4)]
    mend = [1, 2, 3, 4, 4.8, 9.7, 10.7, 11.7, 12.7]
    links, arrives, program = {}, {}, []
    for name, items, ends, dev, ssem, rsem in (
        ("x", xl, xend, twin, xs, xr), ("p", pp, pend, pal, ps, pr), ("m", ml, mend, near, ms, mr),
    ):
        links[name] = []
        for i, (tag, made, src, dst) in enumerate(items):
            c = pltpu.make_async_remote_copy(
                src, dst, ssem.at[i], rsem.at[i], device_id=dev, device_id_type=MESH
            )
            links[name].append((tag, c))
            arrives[tag] = c
            free = ends[i - DEPTH] if i >= DEPTH else 0.0
            program.append((max(free, made), name, i))
    pair = [
        pltpu.make_async_remote_copy(
            mine.at[i], far.at[i], fs.at[i], fr.at[i], device_id=partner, device_id_type=MESH
        )
        for i in range(2)
    ]
    seen, ready = set(), set()

    def need(*tag):
        if tag not in seen:
            seen.add(tag)
            arrives[tag].wait_recv()

    def widen(x):
        return x.astype(F32)

    def prepare(link, tag):
        kind, j, q = tag
        if kind == "w" and j == 3:
            need("w", 1, q)
        if kind == "v":
            need("w", 2, q)
        if kind == "rx":
            assert ("sums", 2 + j) in ready
        if kind == "b":
            assert ("back", j) in ready
        if kind == "k":
            assert "keys" in ready
        if kind == "zf":
            assert ("sums", 1) in ready
            need("rx", 1, q)

            @pl.loop(0, n4 // 32)
            def _(m):
                r = pl.ds(pl.multiple_of(q * n4 + m * 32, 32), 32)
                part[0, r, :] = (widen(part[0, r, :]) + widen(rx[1, r, :])).astype(BF16)

    def issue(link, i):
        tag, c = links[link][i]
        if i >= DEPTH:
            links[link][i - DEPTH][1].wait_send()
        prepare(link, tag)
        c.start()

    def sums(slot):
        need("c", 0, 0)
        need("c", 0, 1)
        need("t", slot, 0)
        c = cols_of(slot)
        if slot == 0:
            assert "base" in ready

        @pl.loop(0, Q)
        def _(q):
            qc = pl.ds(pl.multiple_of(q * wide, 128), wide)
            g = lax.dot_general(tok[:, c], cot[:, qc], TN, preferred_element_type=F32)
            g = g + lax.dot_general(tokp[slot], cotp[:, qc], TN, preferred_element_type=F32)
            if slot:
                part[slot - 1, :, qc] = (g * scale).astype(BF16)
            else:
                trk[:, qc] += g * scale

        ready.add(("sums", slot))

    def add_rows(kind, i):
        assert "base" in ready
        need(kind, 0, i)
        src = rx.at[0] if kind == "rx" else zf

        @pl.loop(0, n4 // 32)
        def _(m):
            r = pl.ds(pl.multiple_of(i * n4 + m * 32, 32), 32)
            trk[r, :] += widen(src[r, :])

    def weights(slot):
        if slot:
            for q in range(Q):
                need("w", slot, q)
        if slot == 3:
            need("v", 3, 3)

    def grad_of(c_ref, slot, store):
        @pl.loop(0, 2)
        def _(m):
            r = pl.ds(pl.multiple_of(m * half, half), half)
            t = lax.dot_general(c_ref[r, col(0)], w[slot, 0], NT, preferred_element_type=F32)
            for q in range(1, Q):
                t = t + lax.dot_general(c_ref[r, col(q)], w[slot, q], NT, preferred_element_type=F32)
            store(r, t.astype(BF16))

    def keys_of(total, slot, read):
        @pl.loop(0, Q)
        def _(q):
            qc = pl.ds(pl.multiple_of(q * wide, 128), wide)
            t = jnp.dot(read(), w[slot, q], preferred_element_type=F32)
            if slot == 0:
                total[:, qc] = t
            else:
                total[:, qc] += t

    def own(slot):
        weights(slot)
        c = cols_of(slot)
        keys_of(acc, slot, lambda: tok[:, c])

        def store(r, v):
            back[r, c] = v

        grad_of(cot, slot, store)

    def pals_back(slot):
        weights(slot)
        need("c", 0, 0)
        need("c", 0, 1)

        def store(r, v):
            backp[slot, r, :] = v

        grad_of(cotp, slot, store)
        ready.add(("back", slot))

    def pals_keys(slot):
        weights(slot)
        need("t", slot, 0)
        keys_of(accp, slot, lambda: tokp[slot])

    def by_rows(f):
        n = toks // 8

        @pl.loop(0, 8)
        def _(i):
            f(pl.ds(pl.multiple_of(i * n, n), n))

    def pals_keys_out():
        def f(r):
            keysp[r, :] = accp[r, :].astype(BF16)

        by_rows(f)
        ready.add("keys")

    def keys_out():
        need("k", 0, 0)

        def f(r):
            keys[r, :] = (acc[r, :] + widen(keysi[r, :])).astype(BF16)

        by_rows(f)

    def send_pair():
        loads["trk"].wait()

        @pl.loop(0, rows // 32)
        def _(i):
            r = pl.ds(pl.multiple_of(i * 32, 32), 32)
            t = trk[r, :]
            mine[0, r, :] = (par[r, :] - 0.01 * t).astype(BF16)
            mine[1, r, :] = t.astype(BF16)

        pair[0].start()
        pair[1].start()

    def average():
        loads["old"].wait()
        pair[0].wait_recv()
        pair[1].wait_recv()

        @pl.loop(0, rows // 32)
        def _(i):
            r = pl.ds(pl.multiple_of(i * 32, 32), 32)
            t = trk[r, :]
            par[r, :] = 0.5 * ((par[r, :] - 0.01 * t) + widen(far[0, r, :]))
            trk[r, :] = 0.5 * (t + widen(far[1, r, :])) - old[r, :]

        ready.add("base")

    def cast(q):
        loads[q].wait()
        w[0, q] = par[:, col(q)].astype(BF16)

    loads["cot"].wait()
    cast(0)
    pl.semaphore_wait(barrier, 4)
    issue("p", 0)
    issue("x", 0)
    issue("m", 0)
    issue("p", 1)
    for q in range(1, Q):
        cast(q)
        if q < DEPTH:
            issue("x", q)
            issue("m", q)
    loads["tok"].wait()

    jobs = [
        (0.1, send_pair),
        (0.6, lambda: own(0)),
        (3.5, lambda: pals_back(0)),
        (4.3, lambda: pals_back(1)),
        (4.6, lambda: pals_back(2)),
        (4.9, lambda: sums(3)),
        (5.8, lambda: sums(2)),
        (6.3, lambda: own(1)),
        (6.7, lambda: sums(1)),
        (7.1, lambda: own(2)),
        (7.7, lambda: (pals_keys(0), pals_keys(1), pals_keys(2))),
        (8.1, lambda: (pals_back(3), pals_keys(3), pals_keys_out())),
        (9.2, average),
        (9.3, lambda: sums(0)),
        (10.0, lambda: own(3)),
        (12.7, lambda: add_rows("rx", 0)),
        (13.5, lambda: (add_rows("zf", 0), add_rows("zf", 1))),
        (13.7, lambda: (add_rows("rx", 1), add_rows("zf", 2), add_rows("zf", 3))),
        (14.6, keys_out),
        (14.7, lambda: add_rows("rx", 2)),
    ]
    started = {"x": DEPTH, "p": 2, "m": DEPTH}
    order = [(key, 0, name, i) for key, name, i in program if i >= started[name]]
    order += [(key, 1, "", job) for key, job in jobs]
    for key, kind, name, what in sorted(order, key=lambda e: e[:3]):
        if kind:
            what()
        else:
            issue(name, what)
    add_rows("rx", 3)

    for name, items in links.items():
        for tag, c in items:
            if tag not in seen:
                seen.add(tag)
                c.wait_recv()
        for tag, c in items[-DEPTH:]:
            c.wait_send()
    for c in pair:
        c.wait_send()


def write_out(keys, back, par, trk, keys_h, back_h, par_h, trk_h, done):
    copies = []
    for src, dst in ((back, back_h), (par, par_h), (trk, trk_h), (keys, keys_h)):
        n = src.shape[0] // 4
        for i in range(4):
            r = pl.ds(i * n, n)
            copies.append(pltpu.make_async_copy(src.at[r], dst.at[0, r], done.at[len(copies)]))
    for c in copies:
        c.start()
    for c in copies:
        c.wait()


def call(level, tokens, cotangent, params, tracker, grad_old):
    _, toks, d = tokens.shape
    _, rows, kv = params.shape
    wide = kv // Q
    scale = 1.0 / float(toks * 2 * NZ) ** 0.5
    sem = pltpu.SemaphoreType.DMA
    hbm = pl.BlockSpec(memory_space=pltpu.HBM)
    vmem = pl.BlockSpec(memory_space=pltpu.VMEM)
    results = pl.pallas_call(
        functools.partial(kernel, level, scale),
        out_shape=(
            pltpu.VMEM((toks, kv), BF16),
            pltpu.VMEM((toks, d), BF16),
            pltpu.VMEM((rows, kv), F32),
            pltpu.VMEM((rows, kv), F32),
        ),
        in_specs=[hbm] * 5,
        out_specs=(vmem,) * 4,
        scratch_shapes=[
            pltpu.VMEM((toks, d), BF16),
            pltpu.VMEM((toks, kv), BF16),
            pltpu.VMEM((rows, kv), F32),
            pltpu.VMEM((4, Q, rows, wide), BF16),
            pltpu.VMEM((3, rows, kv), BF16),
            pltpu.VMEM((4, toks, rows), BF16),
            pltpu.VMEM((toks, kv), BF16),
            pltpu.VMEM((2, rows, kv), BF16),
            pltpu.VMEM((rows, kv), BF16),
            pltpu.VMEM((2, rows, kv), BF16),
            pltpu.VMEM((2, rows, kv), BF16),
            pltpu.VMEM((toks, kv), F32),
            pltpu.VMEM((toks, kv), F32),
            pltpu.VMEM((4, toks, rows), BF16),
            pltpu.VMEM((toks, kv), BF16),
            pltpu.VMEM((toks, kv), BF16),
            sem((Q + 4,)),
            sem((16,)), sem((16,)), sem((11,)), sem((11,)), sem((9,)), sem((9,)), sem((2,)), sem((2,)),
        ],
        compiler_params=pltpu.CompilerParams(
            collective_id=level, has_side_effects=True, vmem_limit_bytes=50 << 20
        ),
        cost_estimate=pl.CostEstimate(
            flops=6 * toks * d * kv, bytes_accessed=14 << 20, transcendentals=0
        ),
        name=f"train_step_{level}",
    )(tokens, cotangent, params, tracker, grad_old)
    return pl.pallas_call(
        write_out,
        out_shape=(
            jax.ShapeDtypeStruct(cotangent.shape, BF16),
            jax.ShapeDtypeStruct(tokens.shape, BF16),
            jax.ShapeDtypeStruct(params.shape, F32),
            jax.ShapeDtypeStruct(params.shape, F32),
        ),
        in_specs=[vmem] * 4,
        out_specs=(hbm,) * 4,
        scratch_shapes=[sem((16,))],
        compiler_params=pltpu.CompilerParams(vmem_limit_bytes=1 << 20),
        name="write_out",
    )(*[pltpu.with_memory_space_constraint(r, pltpu.VMEM) for r in results])


def on_device(tokens, cotangent, params, tracker, grad_old, step):
    branches = [functools.partial(call, level) for level in range(3)]
    return lax.switch(
        step[0], branches, tokens, cotangent, params, tracker, grad_old
    )


def solution(mesh):
    rows = P("rep", "tp", None)
    return jax.shard_map(
        on_device,
        mesh=mesh,
        in_specs=(rows,) * 5 + (P(),),
        out_specs=(rows,) * 4,
        check_vma=False,
    )
```

time: 137 us -> 125 us (0.912)
  Pallas kernels: 135 us -> 123 us
    pallas_call x1, Pallas kernels: 131 us -> 118 us  [call(): pl.pallas_call(functools.partial(kernel, level, scale), out_shape=(pltpu....]
where the time goes in v3:
time: 125 us
  Pallas kernels  123 us (98%)
  between operations  1.48 us (1%)
    pallas_call x1, Pallas kernels, call(): pl.pallas_call(functools.partial(kernel, level, scale), out_shape=(pltpu....  118 us
    pallas_call x1, Pallas kernels, call(): pl.pallas_call(write_out, out_shape=(jax.ShapeDtypeStruct(cotangent.shape...  4.38 us

profile of v3, /device:TPU:1, one launch (start us, length us, event | category | flops | bytes accessed | tf_op | source)
XLA Modules:
  0.0 124.7 jit_solution(11128768484654211433)
XLA Ops:
  1.3 123.2 %conditional.1 = ((bf16[1,512,1024]{2,1,0:T(8,128)(2,1)}, bf16[1,512,5120]{2,1,0:T(8,128)(2,1)}, f32[1,640,1024]{2,1,0:T(8,128)}, f32[1,640,1024]{2,1,0:T(8,128)})) conditional(s32[]{:T(128)} %bitcast, (bf16[1,512,5120]{2,1,0:T(8,128)(2,1)}, bf16[1,512,1024]{2,1,0:T(8,128)(2,1)}, f32[1,640,1024]{2,1,0:T(8,128)}, ...), branch_computations={%region_0.0_spmd, %region_1.0_spmd, %region_2.0_spmd} | conditional | flops 16106127360 | bytes 14680072 | solution.py:412
  1.7 118.1 %train_step_2.1 = (bf16[512,1024]{1,0:T(8,128)(2,1)S(1)}, bf16[512,5120]{1,0:T(8,128)(2,1)S(1)}, f32[640,1024]{1,0:T(8,128)S(1)}, f32[640,1024]{1,0:T(8,128)S(1)}) custom-call(bf16[1,512,5120]{2,1,0:T(8,128)(2,1)} %get-tuple-element.48.tok_h, bf16[1,512,1024]{2,1,0:T(8,128)(2,1)} %get-tuple-element.49.cot_h, f32[1,640,1024]{2,1,0:T(8,128)} %get-tuple-element.50.par_h, ...), custom_call_target="tpu_custom_call" | custom-call | flops 16106127360 | bytes 14680064 | tf_op jit(solution)/shard_map/cond/branch_2_fun/train_step_2/pallas_call | solution.py:356
  119.8 4.4 %write_out.5 = (bf16[1,512,1024]{2,1,0:T(8,128)(2,1)}, bf16[1,512,5120]{2,1,0:T(8,128)(2,1)}, f32[1,640,1024]{2,1,0:T(8,128)}, f32[1,640,1024]{2,1,0:T(8,128)}) custom-call(bf16[512,1024]{1,0:T(8,128)(2,1)S(1)} %get-tuple-element.53.keys, bf16[512,5120]{1,0:T(8,128)(2,1)S(1)} %get-tuple-element.54.back, f32[640,1024]{1,0:T(8,128)S(1)} %get-tuple-element.55.par, ...), custom_call_target="tpu_custom_call" | custom-call | tf_op jit(solution)/shard_map/cond/branch_2_fun/write_out/pallas_call | solution.py:394

commit v4 on v3

--- a/solution.py
+++ b/solution.py
@@ -17,25 +17,26 @@
 
 
 def kernel(
-    level, scale,
-    tok_h, cot_h, par_h, trk_h, old_h,
+    scale,
+    tok_h, cot_h, par_h, trk_h, old_h, step_h,
     keys, back, par, trk,
     tok, cot, old, w, part, tokp, cotp, rx, zf, mine, far, acc, accp, backp, keysp, keysi,
-    load, xs, xr, ps, pr, ms, mr, fs, fr,
+    which, load, xs, xr, ps, pr, ms, mr, ys, yr, fs, fr, cs, cr,
 ):
     rep, tp = lax.axis_index("rep"), lax.axis_index("tp")
     line, z = lax.div(tp, NZ), lax.rem(tp, NZ)
     toks = tok.shape[0]
     rows, kv = par.shape
     wide = kv // Q
-    stride = 2**level
-    bit = lax.rem(lax.div(rep, stride), 2)
     step = 1 - 2 * lax.rem(z + rep, 2)
     zp, zi = lax.rem(z + step + NZ, NZ), lax.rem(z - step + NZ, NZ)
     twin = (rep, lax.rem(tp + NZ, 2 * NZ))
     pal = (rep, line * NZ + zp)
     near = (rep, line * NZ + zi)
-    partner = (rep + stride * (1 - 2 * bit), tp)
+    y = lax.rem(lax.div(rep, 2), 4)
+    mate = (rep + 1 - 2 * lax.rem(rep, 2), tp)
+    beside = (rep + 2 * (1 - 2 * lax.rem(y, 2)), tp)
+    across = (rep + 2 * (3 - 2 * y), tp)
 
     def col(q):
         return pl.ds(q * wide, wide)
@@ -45,17 +46,18 @@
         owner = lax.rem(line + slot // 2, 2) * NZ + (b if slot % 2 else a)
         return pl.ds(pl.multiple_of(owner * rows, 128), rows)
 
-    barrier = pltpu.get_barrier_semaphore()
-    for other in (twin, pal, near, partner):
-        pl.semaphore_signal(barrier, 1, device_id=other, device_id_type=MESH)
     loads = {"cot": pltpu.make_async_copy(cot_h.at[0], cot, load.at[0])}
     for q in range(Q):
         loads[q] = pltpu.make_async_copy(par_h.at[0, :, col(q)], par.at[:, col(q)], load.at[1 + q])
     loads["tok"] = pltpu.make_async_copy(tok_h.at[0], tok, load.at[Q + 1])
     loads["trk"] = pltpu.make_async_copy(trk_h.at[0], trk, load.at[Q + 2])
     loads["old"] = pltpu.make_async_copy(old_h.at[0], old, load.at[Q + 3])
-    for c in loads.values():
-        c.start()
+    loads["step"] = pltpu.make_async_copy(step_h, which, load.at[Q + 4])
+    loads[0].start()
+    loads["cot"].start()
+    barrier = pltpu.get_barrier_semaphore()
+    for other in (twin, pal, near, mate, beside, across):
+        pl.semaphore_signal(barrier, 1, device_id=other, device_id_type=MESH)
 
     half, n4 = toks // 2, rows // 4
     cut = rows // 2
@@ -83,9 +85,19 @@
     ml += [(("v", 3, 3), 4.3, w.at[2, 3, hi], w.at[3, 3, hi])]
     ml += [(("zf", 0, i), 8.7 + i, part.at[0, quarter(i)], zf.at[quarter(i)]) for i in range(4)]
     mend = [1, 2, 3, 4, 4.8, 9.7, 10.7, 11.7, 12.7]
+    both = [(a, i) for a in range(2) for i in range(4)]
+    yl = [(("y", a, i), 0.15, mine.at[a, quarter(i)], far.at[1, a, quarter(i)]) for a, i in both]
+    yend = [n + 1.2 for n in range(8)]
+    fl = [
+        (("f", a, i), 4 * a + i + 1.4, far.at[1, a, quarter(i)], far.at[2, a, quarter(i)])
+        for a, i in both
+    ]
+    fend = [n + 2.4 for n in range(8)]
+    cl = [(("o", a, 0), 0.15, mine.at[a], far.at[0, a]) for a in range(2)]
     links, arrives, program = {}, {}, []
     for name, items, ends, dev, ssem, rsem in (
         ("x", xl, xend, twin, xs, xr), ("p", pp, pend, pal, ps, pr), ("m", ml, mend, near, ms, mr),
+        ("y", yl, yend, beside, ys, yr), ("f", fl, fend, across, fs, fr), ("o", cl, [1, 2], mate, cs, cr),
     ):
         links[name] = []
         for i, (tag, made, src, dst) in enumerate(items):
@@ -96,12 +108,6 @@
             arrives[tag] = c
             free = ends[i - DEPTH] if i >= DEPTH else 0.0
             program.append((max(free, made), name, i))
-    pair = [
-        pltpu.make_async_remote_copy(
-            mine.at[i], far.at[i], fs.at[i], fr.at[i], device_id=partner, device_id_type=MESH
-        )
-        for i in range(2)
-    ]
     seen, ready = set(), set()
 
     def need(*tag):
@@ -122,6 +128,10 @@
             assert ("sums", 2 + j) in ready
         if kind == "b":
             assert ("back", j) in ready
+        if kind in ("y", "o"):
+            assert "mine" in ready
+        if kind == "f":
+            need("y", j, q)
         if kind == "k":
             assert "keys" in ready
         if kind == "zf":
@@ -254,20 +264,31 @@
             mine[0, r, :] = (par[r, :] - 0.01 * t).astype(BF16)
             mine[1, r, :] = t.astype(BF16)
 
-        pair[0].start()
-        pair[1].start()
+        ready.add("mine")
 
     def average():
         loads["old"].wait()
-        pair[0].wait_recv()
-        pair[1].wait_recv()
+        loads["step"].wait()
+        for a, i in both:
+            need("y", a, i)
+            need("f", a, i)
+        need("o", 0, 0)
+        need("o", 1, 0)
+        k = which[0]
+        one = [
+            jnp.where(k <= 0, 1.0, 0.0), jnp.where(k == 1, 1.0, 0.0), jnp.where(k >= 2, 1.0, 0.0),
+        ]
+
+        def partners(a, r):
+            t = one[0] * widen(far[0, a, r, :]) + one[1] * widen(far[1, a, r, :])
+            return t + one[2] * widen(far[2, a, r, :])
 
         @pl.loop(0, rows // 32)
         def _(i):
             r = pl.ds(pl.multiple_of(i * 32, 32), 32)
             t = trk[r, :]
-            par[r, :] = 0.5 * ((par[r, :] - 0.01 * t) + widen(far[0, r, :]))
-            trk[r, :] = 0.5 * (t + widen(far[1, r, :])) - old[r, :]
+            par[r, :] = 0.5 * ((par[r, :] - 0.01 * t) + partners(0, r))
+            trk[r, :] = 0.5 * (t + partners(1, r)) - old[r, :]
 
         ready.add("base")
 
@@ -275,13 +296,15 @@
         loads[q].wait()
         w[0, q] = par[:, col(q)].astype(BF16)
 
-    loads["cot"].wait()
     cast(0)
-    pl.semaphore_wait(barrier, 4)
-    issue("p", 0)
+    pl.semaphore_wait(barrier, 6)
     issue("x", 0)
     issue("m", 0)
+    loads["cot"].wait()
+    issue("p", 0)
     issue("p", 1)
+    for name in (1, 2, 3, "trk", "tok", "old", "step"):
+        loads[name].start()
     for q in range(1, Q):
         cast(q)
         if q < DEPTH:
@@ -302,16 +325,16 @@
         (7.1, lambda: own(2)),
         (7.7, lambda: (pals_keys(0), pals_keys(1), pals_keys(2))),
         (8.1, lambda: (pals_back(3), pals_keys(3), pals_keys_out())),
-        (9.2, average),
-        (9.3, lambda: sums(0)),
-        (10.0, lambda: own(3)),
+        (9.2, lambda: own(3)),
+        (11.2, average),
+        (11.3, lambda: sums(0)),
         (12.7, lambda: add_rows("rx", 0)),
         (13.5, lambda: (add_rows("zf", 0), add_rows("zf", 1))),
         (13.7, lambda: (add_rows("rx", 1), add_rows("zf", 2), add_rows("zf", 3))),
         (14.6, keys_out),
         (14.7, lambda: add_rows("rx", 2)),
     ]
-    started = {"x": DEPTH, "p": 2, "m": DEPTH}
+    started = {"x": DEPTH, "p": 2, "m": DEPTH, "y": 0, "f": 0, "o": 0}
     order = [(key, 0, name, i) for key, name, i in program if i >= started[name]]
     order += [(key, 1, "", job) for key, job in jobs]
     for key, kind, name, what in sorted(order, key=lambda e: e[:3]):
@@ -328,15 +351,13 @@
                 c.wait_recv()
         for tag, c in items[-DEPTH:]:
             c.wait_send()
-    for c in pair:
-        c.wait_send()
 
 
 def write_out(keys, back, par, trk, keys_h, back_h, par_h, trk_h, done):
     copies = []
     for src, dst in ((back, back_h), (par, par_h), (trk, trk_h), (keys, keys_h)):
-        n = src.shape[0] // 4
-        for i in range(4):
+        n = src.shape[0] // 2
+        for i in range(2):
             r = pl.ds(i * n, n)
             copies.append(pltpu.make_async_copy(src.at[r], dst.at[0, r], done.at[len(copies)]))
     for c in copies:
@@ -345,7 +366,7 @@
         c.wait()
 
 
-def call(level, tokens, cotangent, params, tracker, grad_old):
+def on_device(tokens, cotangent, params, tracker, grad_old, step):
     _, toks, d = tokens.shape
     _, rows, kv = params.shape
     wide = kv // Q
@@ -354,14 +375,14 @@
     hbm = pl.BlockSpec(memory_space=pltpu.HBM)
     vmem = pl.BlockSpec(memory_space=pltpu.VMEM)
     results = pl.pallas_call(
-        functools.partial(kernel, level, scale),
+        functools.partial(kernel, scale),
         out_shape=(
             pltpu.VMEM((toks, kv), BF16),
             pltpu.VMEM((toks, d), BF16),
             pltpu.VMEM((rows, kv), F32),
             pltpu.VMEM((rows, kv), F32),
         ),
-        in_specs=[hbm] * 5,
+        in_specs=[hbm] * 6,
         out_specs=(vmem,) * 4,
         scratch_shapes=[
             pltpu.VMEM((toks, d), BF16),
@@ -374,23 +395,25 @@
             pltpu.VMEM((2, rows, kv), BF16),
             pltpu.VMEM((rows, kv), BF16),
             pltpu.VMEM((2, rows, kv), BF16),
-            pltpu.VMEM((2, rows, kv), BF16),
+            pltpu.VMEM((3, 2, rows, kv), BF16),
             pltpu.VMEM((toks, kv), F32),
             pltpu.VMEM((toks, kv), F32),
             pltpu.VMEM((4, toks, rows), BF16),
             pltpu.VMEM((toks, kv), BF16),
             pltpu.VMEM((toks, kv), BF16),
-            sem((Q + 4,)),
-            sem((16,)), sem((16,)), sem((11,)), sem((11,)), sem((9,)), sem((9,)), sem((2,)), sem((2,)),
+            pltpu.SMEM((1,), jnp.int32),
+            sem((Q + 5,)),
+            sem((16,)), sem((16,)), sem((11,)), sem((11,)), sem((9,)), sem((9,)),
+            sem((8,)), sem((8,)), sem((8,)), sem((8,)), sem((2,)), sem((2,)),
         ],
         compiler_params=pltpu.CompilerParams(
-            collective_id=level, has_side_effects=True, vmem_limit_bytes=50 << 20
+            collective_id=0, has_side_effects=True, vmem_limit_bytes=50 << 20
         ),
         cost_estimate=pl.CostEstimate(
             flops=6 * toks * d * kv, bytes_accessed=14 << 20, transcendentals=0
         ),
-        name=f"train_step_{level}",
-    )(tokens, cotangent, params, tracker, grad_old)
+        name="train_step",
+    )(tokens, cotangent, params, tracker, grad_old, step)
     return pl.pallas_call(
         write_out,
         out_shape=(
@@ -401,17 +424,10 @@
         ),
         in_specs=[vmem] * 4,
         out_specs=(hbm,) * 4,
-        scratch_shapes=[sem((16,))],
+        scratch_shapes=[sem((8,))],
         compiler_params=pltpu.CompilerParams(vmem_limit_bytes=1 << 20),
         name="write_out",
     )(*[pltpu.with_memory_space_constraint(r, pltpu.VMEM) for r in results])
-
-
-def on_device(tokens, cotangent, params, tracker, grad_old, step):
-    branches = [functools.partial(call, level) for level in range(3)]
-    return lax.switch(
-        step[0], branches, tokens, cotangent, params, tracker, grad_old
-    )
 
 
 def solution(mesh):

time: 125 us -> 124 us (level)
  no operation moved by 1% of the time
where the time goes in v4:
time: 124 us
  Pallas kernels  123 us (99%)
  between operations  1.29 us (1%)
    pallas_call x1, Pallas kernels, on_device(): pl.pallas_call(functools.partial(kernel, scale), out_shape=(pltpu.VMEM((t...  118 us
    pallas_call x1, Pallas kernels, on_device(): pl.pallas_call(write_out, out_shape=(jax.ShapeDtypeStruct(cotangent.shape...  4.33 us

profile of v4, /device:TPU:1, one launch (start us, length us, event | category | flops | bytes accessed | tf_op | source)
XLA Modules:
  0.0 123.9 jit_solution(3787337329766613060)
XLA Ops:
  1.3 118.3 %train_step.1 = (bf16[512,1024]{1,0:T(8,128)(2,1)S(1)}, bf16[512,5120]{1,0:T(8,128)(2,1)S(1)}, f32[640,1024]{1,0:T(8,128)S(1)}, f32[640,1024]{1,0:T(8,128)S(1)}) custom-call(bf16[1,512,5120]{2,1,0:T(8,128)(2,1)} %tok_h.1, bf16[1,512,1024]{2,1,0:T(8,128)(2,1)} %cot_h.1, f32[1,640,1024]{2,1,0:T(8,128)} %par_h.1, f32[1,640,1024]{2,1,0:T(8,128)} %trk_h.1, ...), custom_call_target="tpu_custom_call" | custom-call | flops 16106127360 | bytes 14680064 | tf_op jit(solution)/shard_map/train_step/pallas_call | solution.py:377
  119.6 4.3 %write_out.1 = (bf16[1,512,1024]{2,1,0:T(8,128)(2,1)}, bf16[1,512,5120]{2,1,0:T(8,128)(2,1)}, f32[1,640,1024]{2,1,0:T(8,128)}, f32[1,640,1024]{2,1,0:T(8,128)}) custom-call(bf16[512,1024]{1,0:T(8,128)(2,1)S(1)} %get-tuple-element.8.keys, bf16[512,5120]{1,0:T(8,128)(2,1)S(1)} %get-tuple-element.9.back, f32[640,1024]{1,0:T(8,128)S(1)} %get-tuple-element.10.par, ...), custom_call_target="tpu_custom_call" | custom-call | tf_op jit(solution)/shard_map/write_out/pallas_call | solution.py:417

commit v5 on v4

--- a/solution.py
+++ b/solution.py
@@ -60,7 +60,7 @@
         pl.semaphore_signal(barrier, 1, device_id=other, device_id_type=MESH)
 
     half, n4 = toks // 2, rows // 4
-    cut = rows // 2
+    cut = rows * 9 // 20
     lo, hi = pl.ds(0, cut), pl.ds(cut, rows - cut)
 
     def quarter(i):

time: 124 us -> 124 us (level)
  no operation moved by 1% of the time
where the time goes in v5:
time: 124 us
  Pallas kernels  123 us (99%)
  between operations  1.29 us (1%)
    pallas_call x1, Pallas kernels, on_device(): pl.pallas_call(functools.partial(kernel, scale), out_shape=(pltpu.VMEM((t...  118 us
    pallas_call x1, Pallas kernels, on_device(): pl.pallas_call(write_out, out_shape=(jax.ShapeDtypeStruct(cotangent.shape...  4.33 us

profile of v5, /device:TPU:1, one launch (start us, length us, event | category | flops | bytes accessed | tf_op | source)
XLA Modules:
  0.0 123.9 jit_solution(5091414004547141682)
XLA Ops:
  1.3 118.2 %train_step.1 = (bf16[512,1024]{1,0:T(8,128)(2,1)S(1)}, bf16[512,5120]{1,0:T(8,128)(2,1)S(1)}, f32[640,1024]{1,0:T(8,128)S(1)}, f32[640,1024]{1,0:T(8,128)S(1)}) custom-call(bf16[1,512,5120]{2,1,0:T(8,128)(2,1)} %tok_h.1, bf16[1,512,1024]{2,1,0:T(8,128)(2,1)} %cot_h.1, f32[1,640,1024]{2,1,0:T(8,128)} %par_h.1, f32[1,640,1024]{2,1,0:T(8,128)} %trk_h.1, ...), custom_call_target="tpu_custom_call" | custom-call | flops 16106127360 | bytes 14680064 | tf_op jit(solution)/shard_map/train_step/pallas_call | solution.py:377
  119.5 4.3 %write_out.1 = (bf16[1,512,1024]{2,1,0:T(8,128)(2,1)}, bf16[1,512,5120]{2,1,0:T(8,128)(2,1)}, f32[1,640,1024]{2,1,0:T(8,128)}, f32[1,640,1024]{2,1,0:T(8,128)}) custom-call(bf16[512,1024]{1,0:T(8,128)(2,1)S(1)} %get-tuple-element.8.keys, bf16[512,5120]{1,0:T(8,128)(2,1)S(1)} %get-tuple-element.9.back, f32[640,1024]{1,0:T(8,128)S(1)} %get-tuple-element.10.par, ...), custom_call_target="tpu_custom_call" | custom-call | tf_op jit(solution)/shard_map/write_out/pallas_call | solution.py:417
